TPU v7x, 32 devices: a whole 2x2x4 slice. The times are simulated.
32 devices in a mesh: grp: 2 (over y), tok: 4 (over z), blk: 4 (over x, core).
Axes of the slice: x: 2, y: 2, z: 4, core: 2. Of those that a mesh axis runs over, the one named last changes fastest.
Arguments:
- student: bfloat16 [16384, 2048], P(('grp', 'tok', 'blk')), parts along dimension 0, may hold values from -6 to 6
- teacher: bfloat16 [512, 2048], P(('grp', 'blk'), 'tok'), parts along dimension 0, may hold values from -6 to 6
- student_mask: int32 [16384], P(('grp', 'tok', 'blk')), parts along dimension 0, may hold values from 0 to 1, as said below
- teacher_mask: int32 [512], P(('grp', 'blk')), parts along dimension 0, may hold values from 0 to 1, as said below
Outputs:
- targets: bfloat16 [16384, 2048], P(('grp', 'tok', 'blk')), parts along dimension 0
- potential: float32 [16384], P(('grp', 'tok', 'blk')), parts along dimension 0
There are 2 independent parts, one for each index of `grp`. A program takes and returns all parts, laid end to end along the dimension named above; each array names one. Nothing has to cross between parts.
Inputs may be any that keep to these rules, and one draw needn't show every extreme that they name: `student_mask`: each aligned block of 512 positions holds ones on a prefix of 128 to 512 positions and zeros after it; the last block is all ones. `teacher_mask`: each aligned block of 64 positions holds ones on a prefix of 16 to 64 positions and zeros after it; the last block is all ones.
All inputs are finite; a program needn't handle non-finite values.
Results may differ from a plain program's by a relative error of at most 0.0045.
Values may be sent and summed in bfloat16 or wider, within the bound.
A program may use at most 64 MiB of HBM per device.

v0:
```python
import math

import jax
import jax.numpy as jnp
from jax import lax
from jax.sharding import PartitionSpec as P

ITERS = 3


EPS = 0.25
NEG = -1e30
CONTRACT = (((1,), (1,)), ((), ()))


def joined(part, axis, combine):
    gathered = jax.tree.map(lambda a: lax.all_gather(a, axis), part)

    def take(source):
        return jax.tree.map(lambda a: lax.dynamic_index_in_dim(a, source, 0, False), gathered)

    return lax.fori_loop(
        1, lax.axis_size(axis), lambda source, state: combine(state, take(source)), take(0)
    )


def pair_scores(left, right):
    return lax.dot_general(left, right, CONTRACT, preferred_element_type=jnp.float32)


def combine_pair(first, second):
    top = jnp.maximum(first[0], second[0])
    total = first[1] * jnp.exp(first[0] - top) + second[1] * jnp.exp(second[0] - top)
    return (top, total)


def row_update(scores, column_terms):
    row = scores + column_terms[None, :]
    top = jnp.max(row, axis=1)
    return -EPS * (top + jnp.log(jnp.sum(jnp.exp(row - top[:, None]), axis=1)))


def column_local(scores, potential, log_valid):
    column = scores + (potential / EPS + log_valid)[:, None]
    top = jnp.max(column, axis=0)
    return (top, jnp.sum(jnp.exp(column - top[None, :]), axis=0))


def shards(student, teacher, student_mask, teacher_mask):
    scale = 1.0 / (math.sqrt(student.shape[1]) * EPS)
    teacher_valid = lax.all_gather(teacher_mask, "blk", axis=0, tiled=True)
    by_rows = lax.all_gather(teacher, "blk", axis=0, tiled=True)
    raw = pair_scores(student, lax.all_gather(by_rows, "tok", axis=1, tiled=True))
    scores = raw * scale
    teacher_total = jnp.sum(teacher_valid).astype(jnp.float32)
    log_teacher = jnp.where(teacher_valid > 0, -jnp.log(teacher_total), NEG)
    valid_student = student_mask > 0
    log_student = jnp.where(valid_student, 0.0, NEG).astype(jnp.float32)
    local_count = jnp.sum(student_mask).astype(jnp.float32)
    potential = row_update(scores, log_teacher)
    top, total = column_local(scores, potential, log_student)
    count = lax.psum(local_count, ("tok", "blk"))
    top, total = joined((top, total), ("tok", "blk"), combine_pair)
    log_count = jnp.log(count)
    dual = -EPS * (top + jnp.log(total) - log_count)
    for step in range(ITERS - 1):
        potential = row_update(scores, dual / EPS + log_teacher)
        top, total = column_local(scores, potential, log_student)
        top, total = joined((top, total), ("tok", "blk"), combine_pair)
        dual = -EPS * (top + jnp.log(total) - log_count)
    exponent = scores + (potential / EPS)[:, None] + (dual / EPS + log_teacher)[None, :]
    weights = jnp.where(valid_student[:, None], jnp.exp(exponent), 0.0).astype(jnp.bfloat16)
    summed = jnp.dot(
        weights,
        lax.all_gather(by_rows, "tok", axis=1, tiled=True),
        preferred_element_type=jnp.float32,
    )
    return (summed.astype(jnp.bfloat16), potential)


def solution(mesh):
    in_specs = (
        P(("grp", "tok", "blk"), None),
        P(("grp", "blk"), "tok"),
        P(("grp", "tok", "blk")),
        P(("grp", "blk")),
    )
    out_specs = (P(("grp", "tok", "blk"), None), P(("grp", "tok", "blk")))
    return jax.shard_map(shards, mesh=mesh, in_specs=in_specs, out_specs=out_specs, check_vma=False)
```

profile of v0, /device:TPU:0, one launch (start us, length us, event | category | flops | bytes accessed | tf_op | source)
XLA Modules:
  0.0 187.5 jit_solution(6604000222572540641)
XLA Ops:
  7.2 0.0 copy-start
  7.2 0.0 all-gather.14.cloned.1.call-start
  7.2 8.9 %all_gather.46 = bf16[256,512]{1,0:T(8,128)(2,1)} all-gather(bf16[64,512]{1,0:T(8,128)(2,1)} %param.11), channel_id=1, replica_groups=mesh['grp'=2,'tok'=4,'blk'=4] {'blk'}, dimensions={0}, use_global_device_ids=true | all-gather | bytes 327680 | tf_op jit(solution)/shard_map/all_gather | solution.py:52
  16.2 0.0 all-gather.14.cloned.1.call-update
  16.2 1.3 reduce_sum.75
  18.2 34.1 %psum.7 = f32[]{:T(128)} all-reduce(f32[]{:T(128)S(6)} %convert_element_type.13), channel_id=1, replica_groups=mesh['grp'=2,'tok'=4,'blk'=4] {'tok','blk'}, use_global_device_ids=true, to_apply=%region_8.9 | all-reduce | flops 1 | bytes 8 | tf_op jit(solution)/shard_map/psum | solution.py:62
  53.0 1.2 dynamic-slice
  54.9 0.9 dynamic-update-slice
  55.7 4.3 %all-reduce = s32[256]{0:T(256)S(1)} all-reduce(s32[256]{0:T(256)S(1)} %dynamic-update-slice), channel_id=1, replica_groups=mesh['grp'=2,'tok'=4,'blk'=4] {'blk'}, use_global_device_ids=true, to_apply=%add | all-reduce | flops 256 | bytes 2048
  60.0 0.6 reduce_sum.72
  61.3 0.0 copy-start.1
  61.3 0.0 all-gather.14.cloned.1.call-done
  61.4 0.0 copy-done
  61.4 2.1 %add_reduce_fusion.5 = (f32[512]{0:T(512)S(1)}, f32[512,256]{1,0:T(8,128)S(1)}) fusion(f32[256]{0:T(256)S(1)} %compare_select_fusion, bf16[512,2048]{1,0:T(8,128)(2,1)S(1)} %copy-done, bf16[256,2048]{1,0:T(8,128)(2,1)} %all-gather.14.cloned.1.call-done), kind=kOutput, calls=%fused_computation.23 | convolution fusion | flops 537263616 | bytes 3673088 | tf_op jit(solution)/shard_map/dot_general | solution.py:28
  63.4 0.2 exponential_reduce_fusion.5
  63.7 0.0 copy-done.1
  63.7 0.1 add_reduce_fusion.4
  63.8 0.2 exponential_reduce_fusion.4
  64.0 18.3 %all-gather.6 = f32[16,1,256]{2,1,0:T(1,128)S(1)} all-gather(f32[1,1,256]{2,1,0:T(1,128)S(1)} %bitcast.70), channel_id=2, replica_groups=mesh['grp'=2,'tok'=4,'blk'=4] {'tok','blk'}, dimensions={0}, use_global_device_ids=true | all-gather | bytes 17408 | tf_op jit(solution)/shard_map/all_gather | solution.py:17
  82.3 17.9 %all-gather.7 = f32[16,1,256]{2,1,0:T(1,128)S(1)} all-gather(f32[1,1,256]{2,1,0:T(1,128)S(1)} %bitcast.73), channel_id=3, replica_groups=mesh['grp'=2,'tok'=4,'blk'=4] {'tok','blk'}, dimensions={0}, use_global_device_ids=true | all-gather | bytes 17408 | tf_op jit(solution)/shard_map/all_gather | solution.py:17
  100.2 0.8 while.51
  101.1 0.2 add_reduce_fusion.3
  101.3 0.2 exponential_reduce_fusion.3
  101.5 0.2 add_reduce_fusion.2
  101.7 0.2 exponential_reduce_fusion.2
  101.9 18.3 %all-gather.8 = f32[16,1,256]{2,1,0:T(1,128)S(1)} all-gather(f32[1,1,256]{2,1,0:T(1,128)S(1)} %bitcast.71), channel_id=4, replica_groups=mesh['grp'=2,'tok'=4,'blk'=4] {'tok','blk'}, dimensions={0}, use_global_device_ids=true | all-gather | bytes 17408 | tf_op jit(solution)/shard_map/all_gather | solution.py:17
  120.1 17.9 %all-gather.9 = f32[16,1,256]{2,1,0:T(1,128)S(1)} all-gather(f32[1,1,256]{2,1,0:T(1,128)S(1)} %bitcast.74), channel_id=5, replica_groups=mesh['grp'=2,'tok'=4,'blk'=4] {'tok','blk'}, dimensions={0}, use_global_device_ids=true | all-gather | bytes 17408 | tf_op jit(solution)/shard_map/all_gather | solution.py:17
  138.1 0.8 while.52
  138.9 0.2 add_reduce_fusion.1
  139.1 0.2 exponential_reduce_fusion.1
  139.3 0.6 select_add_fusion
  139.9 0.1 add_reduce_fusion
  140.1 0.2 exponential_reduce_fusion
  140.3 18.3 %all-gather.10 = f32[16,1,256]{2,1,0:T(1,128)S(1)} all-gather(f32[1,1,256]{2,1,0:T(1,128)S(1)} %bitcast.72), channel_id=6, replica_groups=mesh['grp'=2,'tok'=4,'blk'=4] {'tok','blk'}, dimensions={0}, use_global_device_ids=true | all-gather | bytes 17408 | tf_op jit(solution)/shard_map/all_gather | solution.py:17
  158.5 17.9 %all-gather.11 = f32[16,1,256]{2,1,0:T(1,128)S(1)} all-gather(f32[1,1,256]{2,1,0:T(1,128)S(1)} %bitcast.75), channel_id=7, replica_groups=mesh['grp'=2,'tok'=4,'blk'=4] {'tok','blk'}, dimensions={0}, use_global_device_ids=true | all-gather | bytes 17408 | tf_op jit(solution)/shard_map/all_gather | solution.py:17
  176.5 0.8 while.53
  177.3 3.3 %convolution_convert_fusion = bf16[512,2048]{1,0:T(8,128)(2,1)} fusion(bf16[256,2048]{1,0:T(8,128)(2,1)} %all-gather.14.cloned.1.call-done, f32[512,256]{1,0:T(8,128)S(1)} %get-tuple-element.455, f32[256]{0:T(256)S(1)} %multiply_add_fusion.3, f32[512]{0:T(512)S(1)} %get-tuple-element.444, pred[512]{0:T(512)(128)(4,1)S(1)} %get-tuple-element.446), kind=kOutput, calls=%fused_computation.9 | convolution fusion | flops 538443776 | bytes 3673600 | tf_op jit(solution)/shard_map/dot_general | solution.py:73
  (109 shorter events, 1.5 us)
Async XLA Ops:
  7.2 54.2 %copy-start = (bf16[512,2048]{1,0:T(8,128)(2,1)S(1)}, bf16[512,2048]{1,0:T(8,128)(2,1)}, u32[]{:S(2)}) copy-start(bf16[512,2048]{1,0:T(8,128)(2,1)} %param.10) | copy-start | bytes 6291460
  7.2 54.2 %all-gather.14.cloned.1.call-start = ((), (), s32[]{:S(2)}) async-start(), calls=%async_computation | async-start | bytes 1310720 | tf_op jit(solution)/shard_map/all_gather | solution.py:53
  61.3 2.4 %copy-start.1 = (s32[512]{0:T(512)S(1)}, s32[512]{0:T(512)}, u32[]{:S(2)}) copy-start(s32[512]{0:T(512)} %param.12) | copy-start | bytes 6148
Sparse Core Ops, SparseCore 0:
  16.3 28.5 all-gather.13
where the time goes:
time: 188 us
  blocking collectives  156 us (83%)
  between operations  16.8 us (9%)
  other arithmetic  5.56 us (3%)
  matrix products  5.37 us (3%)
  local copies, waits for them, and re-layouts  2.63 us (1%)
    all_gather x6, blocking collectives, joined(): gathered = jax.tree.map(lambda a: lax.all_gather(a, axis), part)  109 us
    psum x1, blocking collectives, shards(): count = lax.psum(local_count, ('tok', 'blk'))  34.1 us
    all_gather x1, blocking collectives, shards(): by_rows = lax.all_gather(teacher, 'blk', axis=0, tiled=True)  8.94 us
    unnamed x1, blocking collectives  4.26 us
  transfers between devices with their start and end apart: 1, of which 0 were waited for; matrix products, arithmetic and copies ran while one was open for 2% of the time, Pallas kernels for 0%

commit v1 on v0

v1 whole, which is shorter than its diff:
```python
import functools
import math

import jax
import jax.numpy as jnp
from jax import lax
from jax.experimental import pallas as pl
from jax.experimental.pallas import tpu as pltpu
from jax.sharding import PartitionSpec as P

ITERS = 3
EPS = 0.25
NEG = -1e30
ROWS = 64
DIRECT = 16


def kernel(
    nt, nb, phases, scale,
    student_hbm, teacher_hbm, student_mask, teacher_mask,
    targets_hbm, potential_ref,
    x_ref, all_t, s_ref, c_ref, lse_ref, o_ref, meta, stats,
    local_sem, out_sem, tok_send, tok_recv, blk_send, blk_recv, meta_send, meta_recv, stat_send, stat_recv,
):
    rows, width = x_ref.shape
    tb, fs = teacher_hbm.shape
    m = nb * tb
    t, b = lax.axis_index("tok"), lax.axis_index("blk")
    bits = [1 << k for k in reversed(range(nb.bit_length() - 1))]

    load_x = pltpu.make_async_copy(student_hbm, x_ref, local_sem.at[0])
    load_x.start()

    def block(c, owner):
        return all_t.at[c, pl.ds(pl.multiple_of(owner * tb, tb), tb), :]

    load_t = pltpu.make_async_copy(teacher_hbm, block(t, b), local_sem.at[1])
    load_t.start()

    def others(axes):
        spans = [range(nt) if "tok" in axes else range(1), range(nb) if "blk" in axes else range(1)]
        return [(i, j) for i in spans[0] for j in spans[1] if i or j]

    def peer(i, j):
        return {"tok": t ^ i, "blk": b ^ j}

    greeted = sorted({p for axes in phases for p in others(axes)} | {p for p in others(("tok",))} | {p for p in others(("blk",))})
    barrier = pltpu.get_barrier_semaphore()
    for i, j in greeted:
        pl.semaphore_signal(barrier, inc=1, device_id=peer(i, j), device_id_type=pl.DeviceIdType.MESH)
    pl.semaphore_wait(barrier, len(greeted))

    def place(axes):
        if len(axes) == 2:
            return t * nb + b
        return t if "tok" in axes else b

    def send_all(ref, send, recv, axes):
        mine = place(axes)
        for i, j in others(axes):
            pltpu.make_async_remote_copy(
                src_ref=ref.at[mine], dst_ref=ref.at[mine], send_sem=send, recv_sem=recv,
                device_id=peer(i, j), device_id_type=pl.DeviceIdType.MESH,
            ).start()

    def wait_bytes(ref, sem):
        pltpu.make_async_copy(ref, ref, sem).wait()

    def arrived(ref, recv, axes):
        wait_bytes(ref.at[pl.ds(0, len(others(axes)))], recv)

    def meta_values():
        ns = jnp.sum(student_mask[...].astype(jnp.float32), axis=1, keepdims=True)
        nteach = jnp.sum(teacher_mask[...].astype(jnp.float32), axis=1, keepdims=True)
        return ns, nteach

    own_students, own_teachers = meta_values()

    def tok_copy(i, source):
        return pltpu.make_async_remote_copy(
            src_ref=teacher_hbm, dst_ref=block(source, b), send_sem=tok_send, recv_sem=tok_recv.at[source],
            device_id=peer(i, 0), device_id_type=pl.DeviceIdType.MESH,
        )

    def blk_copy(c, owner, bit):
        return pltpu.make_async_remote_copy(
            src_ref=block(c, owner), dst_ref=block(c, owner), send_sem=blk_send, recv_sem=blk_recv.at[c, owner],
            device_id=peer(0, bit), device_id_type=pl.DeviceIdType.MESH,
        )

    for i in range(1, nt):
        tok_copy(i, t).start()

    def hold_own(d):
        c = t ^ d
        if isinstance(d, int) and d == 0:
            load_t.wait()
        else:
            tok_copy(0, c).wait_recv()
        for bit in bits:
            blk_copy(c, b, bit).start()

    def forward(d, lowest):
        c = t ^ d
        for h in range(1, nb):
            if (h & -h) != lowest:
                continue
            blk_copy(c, b ^ h, lowest).wait_recv()
            for bit in bits:
                if bit < lowest:
                    blk_copy(c, b ^ h, bit).start()

    hold_own(0)

    meta[0][place(phases[0])] = jnp.concatenate(
        [jnp.broadcast_to(own_students, (1, 128)), jnp.broadcast_to(own_teachers, (1, 128))], axis=1
    )
    send_all(meta[0], meta_send.at[0], meta_recv.at[0], phases[0])

    def multiply(c, columns, first):
        part = lax.dot_general(
            x_ref[:, columns], all_t[c], (((1,), (1,)), ((), ())), preferred_element_type=jnp.float32
        )
        if first:
            s_ref[...] = part
        else:
            s_ref[...] += part

    aligned = fs % 128 == 0 and nt <= 8
    if aligned:
        for d in range(nt + len(bits)):
            if 0 < d < nt:
                hold_own(d)
            for k, bit in enumerate(bits):
                if 0 <= d - k - 1 < nt:
                    forward(d - k - 1, bit)
            done = d - len(bits)
            if 0 <= done < nt:
                if done == 0:
                    load_x.wait()
                c = t ^ done
                multiply(c, pl.ds(pl.multiple_of(c * fs, 128), fs), done == 0)
    else:
        def step(d, carry):
            hold_own(d)
            return carry

        lax.fori_loop(1, nt, step, 0)
        for bit in bits:
            def pass_on(d, carry, bit=bit):
                forward(d, bit)
                return carry

            lax.fori_loop(0, nt, pass_on, 0)
        load_x.wait()
        for c in range(nt):
            multiply(c, pl.ds(c * fs, fs), c == 0)

    arrived(meta[0], meta_recv.at[0], phases[0])
    lane = lax.broadcasted_iota(jnp.int32, (1, m), 1)
    limit = jnp.zeros((1, m), jnp.float32)
    teacher_total = jnp.zeros((1, 1), jnp.float32)
    for j in range(nb):
        slot = t * nb + j if len(phases[0]) == 2 else j
        held = meta[0][slot][:, 128:129]
        teacher_total += held
        limit = jnp.where(lane // tb == j, held, limit)
    valid_teacher = (lane % tb).astype(jnp.float32) < limit
    log_teacher = jnp.where(valid_teacher, -jnp.log(teacher_total), NEG)
    student_total = jnp.sum(meta[0][...][:, :, 0:1], axis=0)
    if len(phases) == 2:
        meta[1][place(phases[1])] = jnp.broadcast_to(student_total, (1, 256))
        send_all(meta[1], meta_send.at[1], meta_recv.at[1], phases[1])
        arrived(meta[1], meta_recv.at[1], phases[1])
        student_total = jnp.sum(meta[1][...][:, :, 0:1], axis=0)
    log_count = jnp.log(student_total)

    def log_sum(values):
        top = jnp.max(values, axis=0)
        return top + jnp.log(jnp.sum(jnp.exp(values - top[None]), axis=0))

    terms = log_teacher
    for it in range(ITERS):
        top = jnp.full((8, m), -jnp.inf, jnp.float32)
        for r in range(0, rows, ROWS):
            s = s_ref[pl.ds(r, ROWS), :]
            if it == 0:
                s = s * scale
                s_ref[pl.ds(r, ROWS), :] = s
            row = s + terms
            high = jnp.max(row, axis=1, keepdims=True)
            lse = high + jnp.log(jnp.sum(jnp.exp(row - high), axis=1, keepdims=True))
            place_in = lax.broadcasted_iota(jnp.int32, (ROWS, 1), 0) + r
            real = place_in.astype(jnp.float32) < own_students
            column = s - lse + jnp.where(real, 0.0, NEG)
            c_ref[pl.ds(r, ROWS), :] = column
            top = jnp.maximum(top, jnp.max(column.reshape(ROWS // 8, 8, m), axis=0))
            if it == ITERS - 1:
                lse_ref[pl.ds(r, ROWS), :] = jnp.broadcast_to(lse, (ROWS, 128))
        top = jnp.max(top, axis=0, keepdims=True)
        total = jnp.zeros((8, m), jnp.float32)
        for r in range(0, rows, ROWS):
            grown = jnp.exp(c_ref[pl.ds(r, ROWS), :] - top)
            total += jnp.sum(grown.reshape(ROWS // 8, 8, m), axis=0)
        partial = top + jnp.log(jnp.sum(total, axis=0, keepdims=True))
        for p, axes in enumerate(phases):
            box = stats[p].at[it]
            box[place(axes)] = partial
            send_all(box, stat_send.at[p, it], stat_recv.at[p, it], axes)
            if it == ITERS - 1 and p == 0:
                potential_ref[...] = (-EPS) * jnp.transpose(lse_ref[...])[0:1, :]
            arrived(box, stat_recv.at[p, it], axes)
            partial = log_sum(box[...])
        terms = (log_count - partial) + log_teacher

    weights = jnp.exp(c_ref[...] + terms).astype(jnp.bfloat16)
    span = width // 4
    if fs % 128:
        for c in range(nt):
            o_ref[:, c * fs : (c + 1) * fs] = jnp.dot(
                weights, all_t[c], preferred_element_type=jnp.float32
            ).astype(jnp.bfloat16)
        store = pltpu.make_async_copy(o_ref, targets_hbm, out_sem.at[0])
        store.start()
        stores = [store]
    else:
        stores = []
        for c in range(nt):
            part = pl.ds(c * fs, fs)
            o_ref[:, part] = jnp.dot(weights, all_t[c], preferred_element_type=jnp.float32).astype(jnp.bfloat16)
            store = pltpu.make_async_copy(o_ref.at[:, part], targets_hbm.at[:, part], out_sem.at[c])
            store.start()
            stores.append(store)

    wait_bytes(all_t.at[pl.ds(0, nt - 1), pl.ds(0, tb), :], tok_send)
    wait_bytes(all_t.at[:, pl.ds(0, (nb - 1) * tb), :], blk_send)
    for p, axes in enumerate(phases):
        arrived(meta[p], meta_send.at[p], axes)
        for it in range(ITERS):
            arrived(stats[p].at[it], stat_send.at[p, it], axes)
    for store in stores:
        store.wait()


def shards(nt, nb, student, teacher, student_mask, teacher_mask):
    rows, width = student.shape
    tb, fs = teacher.shape
    m = nb * tb
    phases = [("tok", "blk")] if nt * nb <= DIRECT else [("blk",), ("tok",)]
    sizes = [math.prod({"tok": nt, "blk": nb}[a] for a in axes) for axes in phases]
    vmem = pl.BlockSpec(memory_space=pltpu.VMEM)
    hbm = pl.BlockSpec(memory_space=pl.ANY)
    dma = pltpu.SemaphoreType.DMA
    targets, potential = pl.pallas_call(
        functools.partial(kernel, nt, nb, phases, 1.0 / (math.sqrt(width) * EPS)),
        out_shape=(
            jax.ShapeDtypeStruct((rows, width), jnp.bfloat16),
            jax.ShapeDtypeStruct((1, rows), jnp.float32),
        ),
        in_specs=[hbm, hbm, vmem, vmem],
        out_specs=(hbm, vmem),
        scratch_shapes=[
            pltpu.VMEM((rows, width), jnp.bfloat16),
            pltpu.VMEM((nt, m, fs), jnp.bfloat16),
            pltpu.VMEM((rows, m), jnp.float32),
            pltpu.VMEM((rows, m), jnp.float32),
            pltpu.VMEM((rows, 128), jnp.float32),
            pltpu.VMEM((rows, width), jnp.bfloat16),
            [pltpu.VMEM((size, 1, 256), jnp.float32) for size in sizes],
            [pltpu.VMEM((ITERS, size, 1, m), jnp.float32) for size in sizes],
            dma((2,)),
            dma((nt,)),
            dma(()),
            dma((nt,)),
            dma(()),
            dma((nt, nb)),
            dma((2,)),
            dma((2,)),
            dma((2, ITERS)),
            dma((2, ITERS)),
        ],
        compiler_params=pltpu.CompilerParams(
            collective_id=0, has_side_effects=True, vmem_limit_bytes=32 * 2**20
        ),
        cost_estimate=pl.CostEstimate(
            flops=4 * rows * m * width, bytes_accessed=4 * rows * width + 2 * m * width, transcendentals=7 * rows * m
        ),
    )(student, teacher, student_mask.reshape(1, rows), teacher_mask.reshape(1, tb))
    return targets, potential.reshape(rows)


def solution(mesh):
    in_specs = (
        P(("grp", "tok", "blk"), None),
        P(("grp", "blk"), "tok"),
        P(("grp", "tok", "blk")),
        P(("grp", "blk")),
    )
    out_specs = (P(("grp", "tok", "blk"), None), P(("grp", "tok", "blk")))
    body = functools.partial(shards, mesh.shape["tok"], mesh.shape["blk"])
    return jax.shard_map(body, mesh=mesh, in_specs=in_specs, out_specs=out_specs, check_vma=False)
```

time: 188 us -> 40.3 us (0.21)
  blocking collectives: 156 us -> 0 us
  Pallas kernels: 0 us -> 33.8 us
  between operations: 16.8 us -> 0.65 us
  other arithmetic: 5.56 us -> 0 us
  matrix products: 5.37 us -> 0 us
  local copies, waits for them, and re-layouts: 2.63 us -> 5.66 us
    all_gather x7 -> x0, blocking collectives: 118 us -> none  [the longest x6 109 us: joined(): gathered = jax.tree.map(lambda a: lax.all_gather(a, axis), part)]
    psum x1 -> x0, blocking collectives: 34.1 us -> none  [shards(): count = lax.psum(local_count, ('tok', 'blk'))]
    pallas_call x0 -> x1, Pallas kernels: none -> 33.8 us  [shards(): pl.pallas_call(functools.partial(kernel, nt, nb, phases, 1.0 / (math.sqrt...]
    dot_general x2 -> x0, matrix products: 5.37 us -> none  [the longest x1 3.32 us: shards(): jnp.dot(weights, lax.all_gather(by_rows, 'tok', axis=1, tiled=True), pref...]
    unnamed x1 -> x0, blocking collectives: 4.26 us -> none
    unnamed x13 -> x10, local copies, waits for them, and re-layouts: 2.13 us -> 5.66 us
    reduce_sum x8 -> x0, other arithmetic: 3.22 us -> none  [the longest x1 1.32 us: shards(): local_count = jnp.sum(student_mask).astype(jnp.float32)]
  transfers between devices with their start and end apart: 1 -> 0, of which waited for: 0 -> 0; matrix products, arithmetic and copies ran while one was open for 2% -> 0% of each run, Pallas kernels for 0% -> 0%
where the time goes in v1:
time: 40.3 us; the launch traced here: 40.1 us
  Pallas kernels  33.8 us (84%)
  local copies, waits for them, and re-layouts  5.66 us (14%)
  between operations  0.65 us (2%)
    pallas_call x1, Pallas kernels, shards(): pl.pallas_call(functools.partial(kernel, nt, nb, phases, 1.0 / (math.sqrt...  33.8 us
    unnamed x10, local copies, waits for them, and re-layouts  5.66 us

profile of v1, /device:TPU:0, one launch (start us, length us, event | category | flops | bytes accessed | tf_op | source)
XLA Modules:
  0.0 40.1 jit_solution(14257142694135915941)
XLA Ops:
  0.6 0.0 copy-start
  0.6 1.6 %copy-done = bf16[512,2048]{1,0:T(8,128)(2,1)S(1)} copy-done((bf16[512,2048]{1,0:T(8,128)(2,1)S(1)}, bf16[512,2048]{1,0:T(8,128)(2,1)}, u32[]{:S(2)}) %copy-start) | copy-done | bytes 2097176
  2.2 0.0 copy-start.1
  2.2 0.8 %copy-done.1 = bf16[64,512]{1,0:T(8,128)(2,1)S(1)} copy-done((bf16[64,512]{1,0:T(8,128)(2,1)S(1)}, bf16[64,512]{1,0:T(8,128)(2,1)}, u32[]{:S(2)}) %copy-start.1) | copy-done | bytes 65560
  3.1 0.0 copy-start.2
  3.1 0.7 %copy-done.2 = s32[512]{0:T(512)S(1)} copy-done((s32[512]{0:T(512)S(1)}, s32[512]{0:T(512)}, u32[]{:S(2)}) %copy-start.2) | copy-done | bytes 2072
  3.7 0.0 copy-start.3
  3.7 0.7 %copy-done.3 = s32[64]{0:T(128)S(1)} copy-done((s32[64]{0:T(128)S(1)}, s32[64]{0:T(128)}, u32[]{:S(2)}) %copy-start.3) | copy-done | bytes 280
  4.4 33.8 %shard_map.59 = (bf16[512,2048]{1,0:T(8,128)(2,1)S(1)}, f32[1,512]{1,0:T(1,128)S(1)}) custom-call(bf16[512,2048]{1,0:T(8,128)(2,1)S(1)} %copy-done, bf16[64,512]{1,0:T(8,128)(2,1)S(1)} %copy-done.1, s32[1,512]{1,0:T(1,128)S(1)} %bitcast.4, s32[1,64]{1,0:T(1,128)S(1)} %bitcast.5), custom_call_target="tpu_custom_call" | custom-call | flops 1073741824 | bytes 5242880 | tf_op jit(solution)/shard_map/pallas_call | solution.py:254
  38.2 1.3 %copy.8 = bf16[512,2048]{1,0:T(8,128)(2,1)} copy(bf16[512,2048]{1,0:T(8,128)(2,1)S(1)} %get-tuple-element.8) | data formatting | bytes 4194304
  39.5 0.6 %copy.9 = f32[512]{0:T(512)} copy(f32[512]{0:T(512)S(1)} %bitcast.3) | data formatting | bytes 4096
Async XLA Ops:
  0.6 1.6 %copy-start = (bf16[512,2048]{1,0:T(8,128)(2,1)S(1)}, bf16[512,2048]{1,0:T(8,128)(2,1)}, u32[]{:S(2)}) copy-start(bf16[512,2048]{1,0:T(8,128)(2,1)} %student_hbm.1) | copy-start | bytes 6291460
  2.2 0.8 %copy-start.1 = (bf16[64,512]{1,0:T(8,128)(2,1)S(1)}, bf16[64,512]{1,0:T(8,128)(2,1)}, u32[]{:S(2)}) copy-start(bf16[64,512]{1,0:T(8,128)(2,1)} %teacher_hbm.1) | copy-start | bytes 196612
  3.1 0.7 %copy-start.2 = (s32[512]{0:T(512)S(1)}, s32[512]{0:T(512)}, u32[]{:S(2)}) copy-start(s32[512]{0:T(512)} %param.6) | copy-start | bytes 6148
  3.7 0.7 %copy-start.3 = (s32[64]{0:T(128)S(1)}, s32[64]{0:T(128)}, u32[]{:S(2)}) copy-start(s32[64]{0:T(128)} %param.7) | copy-start | bytes 772

commit v2 on v1

--- a/solution.py
+++ b/solution.py
@@ -17,9 +17,9 @@
 
 def kernel(
     nt, nb, phases, scale,
-    student_hbm, teacher_hbm, student_mask, teacher_mask,
-    targets_hbm, potential_ref,
-    x_ref, all_t, s_ref, c_ref, lse_ref, o_ref, meta, stats,
+    student_hbm, teacher_hbm, student_mask_hbm, teacher_mask_hbm,
+    column_hbm, copied_t, terms_ref, potential_ref,
+    student_mask, teacher_mask, x_ref, all_t, s_ref, c_ref, lse_ref, meta, stats,
     local_sem, out_sem, tok_send, tok_recv, blk_send, blk_recv, meta_send, meta_recv, stat_send, stat_recv,
 ):
     rows, width = x_ref.shape
@@ -29,6 +29,12 @@
     bits = [1 << k for k in reversed(range(nb.bit_length() - 1))]
 
     load_x = pltpu.make_async_copy(student_hbm, x_ref, local_sem.at[0])
+    load_masks = [
+        pltpu.make_async_copy(student_mask_hbm, student_mask, local_sem.at[2]),
+        pltpu.make_async_copy(teacher_mask_hbm, teacher_mask, local_sem.at[3]),
+    ]
+    for load in load_masks:
+        load.start()
     load_x.start()
 
     def block(c, owner):
@@ -74,7 +80,6 @@
         nteach = jnp.sum(teacher_mask[...].astype(jnp.float32), axis=1, keepdims=True)
         return ns, nteach
 
-    own_students, own_teachers = meta_values()
 
     def tok_copy(i, source):
         return pltpu.make_async_remote_copy(
@@ -112,6 +117,9 @@
 
     hold_own(0)
 
+    for load in load_masks:
+        load.wait()
+    own_students, own_teachers = meta_values()
     meta[0][place(phases[0])] = jnp.concatenate(
         [jnp.broadcast_to(own_students, (1, 128)), jnp.broadcast_to(own_teachers, (1, 128))], axis=1
     )
@@ -155,6 +163,9 @@
         load_x.wait()
         for c in range(nt):
             multiply(c, pl.ds(c * fs, fs), c == 0)
+
+    store_t = pltpu.make_async_copy(all_t, copied_t, out_sem.at[0])
+    store_t.start()
 
     arrived(meta[0], meta_recv.at[0], phases[0])
     lane = lax.broadcasted_iota(jnp.int32, (1, m), 1)
@@ -208,37 +219,52 @@
             box[place(axes)] = partial
             send_all(box, stat_send.at[p, it], stat_recv.at[p, it], axes)
             if it == ITERS - 1 and p == 0:
+                store_c = pltpu.make_async_copy(c_ref, column_hbm, out_sem.at[1])
+                store_c.start()
                 potential_ref[...] = (-EPS) * jnp.transpose(lse_ref[...])[0:1, :]
             arrived(box, stat_recv.at[p, it], axes)
             partial = log_sum(box[...])
         terms = (log_count - partial) + log_teacher
 
-    weights = jnp.exp(c_ref[...] + terms).astype(jnp.bfloat16)
-    span = width // 4
-    if fs % 128:
-        for c in range(nt):
-            o_ref[:, c * fs : (c + 1) * fs] = jnp.dot(
-                weights, all_t[c], preferred_element_type=jnp.float32
-            ).astype(jnp.bfloat16)
-        store = pltpu.make_async_copy(o_ref, targets_hbm, out_sem.at[0])
-        store.start()
-        stores = [store]
-    else:
-        stores = []
-        for c in range(nt):
-            part = pl.ds(c * fs, fs)
-            o_ref[:, part] = jnp.dot(weights, all_t[c], preferred_element_type=jnp.float32).astype(jnp.bfloat16)
-            store = pltpu.make_async_copy(o_ref.at[:, part], targets_hbm.at[:, part], out_sem.at[c])
-            store.start()
-            stores.append(store)
-
+    terms_ref[...] = terms
     wait_bytes(all_t.at[pl.ds(0, nt - 1), pl.ds(0, tb), :], tok_send)
     wait_bytes(all_t.at[:, pl.ds(0, (nb - 1) * tb), :], blk_send)
     for p, axes in enumerate(phases):
         arrived(meta[p], meta_send.at[p], axes)
         for it in range(ITERS):
             arrived(stats[p].at[it], stat_send.at[p, it], axes)
-    for store in stores:
+    store_t.wait()
+    store_c.wait()
+
+
+def average(
+    nt, column_hbm, all_t_hbm, terms_hbm, potential_hbm, targets_hbm, potential_out,
+    c_ref, t_ref, terms_ref, o_ref, in_sem, t_sem, out_sem,
+):
+    fs = t_ref.shape[2]
+    loads = [
+        pltpu.make_async_copy(terms_hbm, terms_ref, in_sem.at[0]),
+        pltpu.make_async_copy(column_hbm, c_ref, in_sem.at[1]),
+    ]
+    blocks = [pltpu.make_async_copy(all_t_hbm.at[c], t_ref.at[c], t_sem.at[c]) for c in range(nt)]
+    pass_on = pltpu.make_async_copy(potential_hbm, potential_out, in_sem.at[2])
+    for load in loads + blocks + [pass_on]:
+        load.start()
+    for load in loads:
+        load.wait()
+    weights = jnp.exp(c_ref[...] + terms_ref[...]).astype(jnp.bfloat16)
+    stores = []
+    for c in range(nt):
+        blocks[c].wait()
+        part = pl.ds(c * fs, fs)
+        o_ref[:, part] = jnp.dot(weights, t_ref[c], preferred_element_type=jnp.float32).astype(jnp.bfloat16)
+        if fs % 128 == 0:
+            stores.append(pltpu.make_async_copy(o_ref.at[:, part], targets_hbm.at[:, part], out_sem.at[c]))
+            stores[-1].start()
+    if not stores:
+        stores.append(pltpu.make_async_copy(o_ref, targets_hbm, out_sem.at[0]))
+        stores[-1].start()
+    for store in stores + [pass_on]:
         store.wait()
 
 
@@ -249,27 +275,30 @@
     phases = [("tok", "blk")] if nt * nb <= DIRECT else [("blk",), ("tok",)]
     sizes = [math.prod({"tok": nt, "blk": nb}[a] for a in axes) for axes in phases]
     vmem = pl.BlockSpec(memory_space=pltpu.VMEM)
-    hbm = pl.BlockSpec(memory_space=pl.ANY)
+    hbm = pl.BlockSpec(memory_space=pltpu.HBM)
     dma = pltpu.SemaphoreType.DMA
-    targets, potential = pl.pallas_call(
+    column, whole_t, terms, potential = pl.pallas_call(
         functools.partial(kernel, nt, nb, phases, 1.0 / (math.sqrt(width) * EPS)),
         out_shape=(
-            jax.ShapeDtypeStruct((rows, width), jnp.bfloat16),
+            jax.ShapeDtypeStruct((rows, m), jnp.float32),
+            jax.ShapeDtypeStruct((nt, m, fs), jnp.bfloat16),
+            jax.ShapeDtypeStruct((1, m), jnp.float32),
             jax.ShapeDtypeStruct((1, rows), jnp.float32),
         ),
-        in_specs=[hbm, hbm, vmem, vmem],
-        out_specs=(hbm, vmem),
+        in_specs=[hbm] * 4,
+        out_specs=(hbm, hbm, vmem, vmem),
         scratch_shapes=[
+            pltpu.VMEM((1, rows), jnp.int32),
+            pltpu.VMEM((1, tb), jnp.int32),
             pltpu.VMEM((rows, width), jnp.bfloat16),
             pltpu.VMEM((nt, m, fs), jnp.bfloat16),
             pltpu.VMEM((rows, m), jnp.float32),
             pltpu.VMEM((rows, m), jnp.float32),
             pltpu.VMEM((rows, 128), jnp.float32),
-            pltpu.VMEM((rows, width), jnp.bfloat16),
             [pltpu.VMEM((size, 1, 256), jnp.float32) for size in sizes],
             [pltpu.VMEM((ITERS, size, 1, m), jnp.float32) for size in sizes],
+            dma((4,)),
             dma((2,)),
-            dma((nt,)),
             dma(()),
             dma((nt,)),
             dma(()),
@@ -280,12 +309,31 @@
             dma((2, ITERS)),
         ],
         compiler_params=pltpu.CompilerParams(
-            collective_id=0, has_side_effects=True, vmem_limit_bytes=32 * 2**20
+            collective_id=0, has_side_effects=True, vmem_limit_bytes=60 * 2**20
         ),
         cost_estimate=pl.CostEstimate(
             flops=4 * rows * m * width, bytes_accessed=4 * rows * width + 2 * m * width, transcendentals=7 * rows * m
         ),
     )(student, teacher, student_mask.reshape(1, rows), teacher_mask.reshape(1, tb))
+    targets, potential = pl.pallas_call(
+        functools.partial(average, nt),
+        out_shape=(
+            jax.ShapeDtypeStruct((rows, width), jnp.bfloat16),
+            jax.ShapeDtypeStruct((1, rows), jnp.float32),
+        ),
+        in_specs=[hbm] * 4,
+        out_specs=(hbm, hbm),
+        scratch_shapes=[
+            pltpu.VMEM((rows, m), jnp.float32),
+            pltpu.VMEM((nt, m, fs), jnp.bfloat16),
+            pltpu.VMEM((1, m), jnp.float32),
+            pltpu.VMEM((rows, width), jnp.bfloat16),
+            dma((3,)),
+            dma((nt,)),
+            dma((nt,)),
+        ],
+        compiler_params=pltpu.CompilerParams(vmem_limit_bytes=60 * 2**20),
+    )(column, whole_t, terms, potential)
     return targets, potential.reshape(rows)
 
 

time: 40.3 us -> 36.6 us (0.908)
  local copies, waits for them, and re-layouts: 5.66 us -> 0 us
  Pallas kernels: 33.8 us -> 35.8 us
    unnamed x10 -> x0, local copies, waits for them, and re-layouts: 5.66 us -> none
    pallas_call x0 -> x1, Pallas kernels: none -> 3.46 us  [shards(): pl.pallas_call(functools.partial(average, nt), out_shape=(jax.ShapeDtypeS...]
    pallas_call x1, Pallas kernels: 33.8 us -> 32.4 us  [shards(): pl.pallas_call(functools.partial(kernel, nt, nb, phases, 1.0 / (math.sqrt...]
where the time goes in v2:
time: 36.6 us; the launch traced here: 36.5 us
  Pallas kernels  35.8 us (98%)
  between operations  0.64 us (2%)
    pallas_call x1, Pallas kernels, shards(): pl.pallas_call(functools.partial(kernel, nt, nb, phases, 1.0 / (math.sqrt...  32.4 us
    pallas_call x1, Pallas kernels, shards(): pl.pallas_call(functools.partial(average, nt), out_shape=(jax.ShapeDtypeS...  3.46 us

profile of v2, /device:TPU:0, one launch (start us, length us, event | category | flops | bytes accessed | tf_op | source)
XLA Modules:
  0.0 36.5 jit_solution(2587195450997029038)
XLA Ops:
  0.6 32.4 %shard_map.59 = (f32[512,256]{1,0:T(8,128)}, bf16[4,256,512]{2,1,0:T(8,128)(2,1)}, f32[1,256]{1,0:T(1,128)}, f32[1,512]{1,0:T(1,128)}) custom-call(bf16[512,2048]{1,0:T(8,128)(2,1)} %student_hbm.1, bf16[64,512]{1,0:T(8,128)(2,1)} %teacher_hbm.1, s32[1,512]{1,0:T(1,128)} %bitcast.3, s32[1,64]{1,0:T(1,128)} %bitcast.5), custom_call_target="tpu_custom_call" | custom-call | flops 1073741824 | bytes 5242880 | tf_op jit(solution)/shard_map/pallas_call | solution.py:280
  33.0 3.5 %shard_map.60 = (bf16[512,2048]{1,0:T(8,128)(2,1)}, f32[1,512]{1,0:T(1,128)}) custom-call(f32[512,256]{1,0:T(8,128)} %get-tuple-element.8.column_hbm, bf16[4,256,512]{2,1,0:T(8,128)(2,1)} %get-tuple-element.9.all_t_hbm, f32[1,256]{1,0:T(1,128)} %get-tuple-element.10.terms_hbm, f32[1,512]{1,0:T(1,128)} %get-tuple-element.11.potential_hbm), custom_call_target="tpu_custom_call" | custom-call | tf_op jit(solution)/shard_map/pallas_call | solution.py:318

commit v3 on v2

--- a/solution.py
+++ b/solution.py
@@ -28,6 +28,22 @@
     t, b = lax.axis_index("tok"), lax.axis_index("blk")
     bits = [1 << k for k in reversed(range(nb.bit_length() - 1))]
 
+    def block(c, owner):
+        return all_t.at[c, pl.ds(pl.multiple_of(owner * tb, tb), tb), :]
+
+    def others(axes):
+        spans = [range(nt) if "tok" in axes else range(1), range(nb) if "blk" in axes else range(1)]
+        return [(i, j) for i in reversed(spans[0]) for j in reversed(spans[1]) if i or j]
+
+    def peer(i, j):
+        return {"tok": t ^ i, "blk": b ^ j}
+
+    greeted = sorted({p for axes in phases for p in others(axes)} | {p for p in others(("tok",))} | {p for p in others(("blk",))})
+    barrier = pltpu.get_barrier_semaphore()
+    for i, j in greeted:
+        pl.semaphore_signal(barrier, inc=1, device_id=peer(i, j), device_id_type=pl.DeviceIdType.MESH)
+    load_t = pltpu.make_async_copy(teacher_hbm, block(t, b), local_sem.at[1])
+    load_t.start()
     load_x = pltpu.make_async_copy(student_hbm, x_ref, local_sem.at[0])
     load_masks = [
         pltpu.make_async_copy(student_mask_hbm, student_mask, local_sem.at[2]),
@@ -36,24 +52,6 @@
     for load in load_masks:
         load.start()
     load_x.start()
-
-    def block(c, owner):
-        return all_t.at[c, pl.ds(pl.multiple_of(owner * tb, tb), tb), :]
-
-    load_t = pltpu.make_async_copy(teacher_hbm, block(t, b), local_sem.at[1])
-    load_t.start()
-
-    def others(axes):
-        spans = [range(nt) if "tok" in axes else range(1), range(nb) if "blk" in axes else range(1)]
-        return [(i, j) for i in spans[0] for j in spans[1] if i or j]
-
-    def peer(i, j):
-        return {"tok": t ^ i, "blk": b ^ j}
-
-    greeted = sorted({p for axes in phases for p in others(axes)} | {p for p in others(("tok",))} | {p for p in others(("blk",))})
-    barrier = pltpu.get_barrier_semaphore()
-    for i, j in greeted:
-        pl.semaphore_signal(barrier, inc=1, device_id=peer(i, j), device_id_type=pl.DeviceIdType.MESH)
     pl.semaphore_wait(barrier, len(greeted))
 
     def place(axes):
@@ -87,21 +85,22 @@
             device_id=peer(i, 0), device_id_type=pl.DeviceIdType.MESH,
         )
 
-    def blk_copy(c, owner, bit):
+    def blk_copy(c, owner, bit, own=False):
         return pltpu.make_async_remote_copy(
-            src_ref=block(c, owner), dst_ref=block(c, owner), send_sem=blk_send, recv_sem=blk_recv.at[c, owner],
+            src_ref=teacher_hbm if own else block(c, owner), dst_ref=block(c, owner), send_sem=blk_send, recv_sem=blk_recv.at[c, owner],
             device_id=peer(0, bit), device_id_type=pl.DeviceIdType.MESH,
         )
 
+    for bit in bits[:1]:
+        blk_copy(t, b, bit, True).start()
     for i in range(1, nt):
         tok_copy(i, t).start()
+    for bit in bits[1:]:
+        blk_copy(t, b, bit, True).start()
 
     def hold_own(d):
         c = t ^ d
-        if isinstance(d, int) and d == 0:
-            load_t.wait()
-        else:
-            tok_copy(0, c).wait_recv()
+        tok_copy(0, c).wait_recv()
         for bit in bits:
             blk_copy(c, b, bit).start()
 
@@ -114,8 +113,6 @@
             for bit in bits:
                 if bit < lowest:
                     blk_copy(c, b ^ h, bit).start()
-
-    hold_own(0)
 
     for load in load_masks:
         load.wait()
@@ -145,6 +142,7 @@
             done = d - len(bits)
             if 0 <= done < nt:
                 if done == 0:
+                    load_t.wait()
                     load_x.wait()
                 c = t ^ done
                 multiply(c, pl.ds(pl.multiple_of(c * fs, 128), fs), done == 0)
@@ -160,6 +158,7 @@
                 return carry
 
             lax.fori_loop(0, nt, pass_on, 0)
+        load_t.wait()
         load_x.wait()
         for c in range(nt):
             multiply(c, pl.ds(c * fs, fs), c == 0)

time: 36.6 us -> 36.3 us (level)
  no operation moved by 1% of the time
where the time goes in v3:
time: 36.3 us; the launch traced here: 36.2 us
  Pallas kernels  35.5 us (98%)
  between operations  0.64 us (2%)
    pallas_call x1, Pallas kernels, shards(): pl.pallas_call(functools.partial(kernel, nt, nb, phases, 1.0 / (math.sqrt...  32.1 us
    pallas_call x1, Pallas kernels, shards(): pl.pallas_call(functools.partial(average, nt), out_shape=(jax.ShapeDtypeS...  3.45 us

profile of v3, /device:TPU:0, one launch (start us, length us, event | category | flops | bytes accessed | tf_op | source)
XLA Modules:
  0.0 36.2 jit_solution(18439578367876390382)
XLA Ops:
  0.6 32.1 %shard_map.59 = (f32[512,256]{1,0:T(8,128)}, bf16[4,256,512]{2,1,0:T(8,128)(2,1)}, f32[1,256]{1,0:T(1,128)}, f32[1,512]{1,0:T(1,128)}) custom-call(bf16[512,2048]{1,0:T(8,128)(2,1)} %student_hbm.1, bf16[64,512]{1,0:T(8,128)(2,1)} %teacher_hbm.1, s32[1,512]{1,0:T(1,128)} %bitcast.3, s32[1,64]{1,0:T(1,128)} %bitcast.5), custom_call_target="tpu_custom_call" | custom-call | flops 1073741824 | bytes 5242880 | tf_op jit(solution)/shard_map/pallas_call | solution.py:279
  32.7 3.4 %shard_map.60 = (bf16[512,2048]{1,0:T(8,128)(2,1)}, f32[1,512]{1,0:T(1,128)}) custom-call(f32[512,256]{1,0:T(8,128)} %get-tuple-element.8.column_hbm, bf16[4,256,512]{2,1,0:T(8,128)(2,1)} %get-tuple-element.9.all_t_hbm, f32[1,256]{1,0:T(1,128)} %get-tuple-element.10.terms_hbm, f32[1,512]{1,0:T(1,128)} %get-tuple-element.11.potential_hbm), custom_call_target="tpu_custom_call" | custom-call | tf_op jit(solution)/shard_map/pallas_call | solution.py:317

commit v4 on v3

--- a/solution.py
+++ b/solution.py
@@ -91,11 +91,9 @@
             device_id=peer(0, bit), device_id_type=pl.DeviceIdType.MESH,
         )
 
-    for bit in bits[:1]:
-        blk_copy(t, b, bit, True).start()
     for i in range(1, nt):
         tok_copy(i, t).start()
-    for bit in bits[1:]:
+    for bit in bits:
         blk_copy(t, b, bit, True).start()
 
     def hold_own(d):

time: 36.3 us -> 36.3 us (level)
  no operation moved by 1% of the time
where the time goes in v4:
time: 36.3 us; the launch traced here: 36.1 us
  Pallas kernels  35.5 us (98%)
  between operations  0.64 us (2%)
    pallas_call x1, Pallas kernels, shards(): pl.pallas_call(functools.partial(kernel, nt, nb, phases, 1.0 / (math.sqrt...  32 us
    pallas_call x1, Pallas kernels, shards(): pl.pallas_call(functools.partial(average, nt), out_shape=(jax.ShapeDtypeS...  3.47 us

profile of v4, /device:TPU:0, one launch (start us, length us, event | category | flops | bytes accessed | tf_op | source)
XLA Modules:
  0.0 36.1 jit_solution(5258093577411864081)
XLA Ops:
  0.6 32.0 %shard_map.59 = (f32[512,256]{1,0:T(8,128)}, bf16[4,256,512]{2,1,0:T(8,128)(2,1)}, f32[1,256]{1,0:T(1,128)}, f32[1,512]{1,0:T(1,128)}) custom-call(bf16[512,2048]{1,0:T(8,128)(2,1)} %student_hbm.1, bf16[64,512]{1,0:T(8,128)(2,1)} %teacher_hbm.1, s32[1,512]{1,0:T(1,128)} %bitcast.3, s32[1,64]{1,0:T(1,128)} %bitcast.5), custom_call_target="tpu_custom_call" | custom-call | flops 1073741824 | bytes 5242880 | tf_op jit(solution)/shard_map/pallas_call | solution.py:277
  32.7 3.5 %shard_map.60 = (bf16[512,2048]{1,0:T(8,128)(2,1)}, f32[1,512]{1,0:T(1,128)}) custom-call(f32[512,256]{1,0:T(8,128)} %get-tuple-element.8.column_hbm, bf16[4,256,512]{2,1,0:T(8,128)(2,1)} %get-tuple-element.9.all_t_hbm, f32[1,256]{1,0:T(1,128)} %get-tuple-element.10.terms_hbm, f32[1,512]{1,0:T(1,128)} %get-tuple-element.11.potential_hbm), custom_call_target="tpu_custom_call" | custom-call | tf_op jit(solution)/shard_map/pallas_call | solution.py:315
